TPU v7x, 32 devices: a whole 2x2x4 slice. The times are simulated.
32 devices in a mesh: case: 4 (over y, x), space: 8 (over z, core).
Axes of the slice: x: 2, y: 2, z: 4, core: 2. Of those that a mesh axis runs over, the one named last changes fastest.
Arguments:
- density: float32 [48, 32, 128], P('space', 'case'), may hold values from 0.3 to 1
- void_depth: int32 [48, 32], P('space', 'case'), may hold values from 0 to 32
- supports: int32 [4, 2], P('case'), may hold values from 1 to 12
- load_x: int32 [4], P('case'), may hold values from 0 to 40
- load_y: int32 [4], P('case'), may hold values from 0 to 24
- load_vectors: float32 [4, 3, 48], P('case'), may hold values from -4 to 4
Outputs:
- displacement: float32 [4, 3, 48, 32, 128], P('case', None, 'space')
- sensitivity: float32 [48, 32, 128], P('space', 'case')
All inputs are finite; a program needn't handle non-finite values.
Results may differ from a plain program's by a relative error of at most 0.0003.
Values sent between devices are 32-bit elements; how exact they have to be, the bound alone decides.
No kernel may reach another device: no remote copies, remote signals or barrier semaphores. Data moves between devices by JAX's collectives and lax.ppermute only.
A program may use at most 64 MiB of HBM per device.

v0:
```python
import math

import jax
import jax.numpy as jnp
from jax import lax
from jax.sharding import PartitionSpec as P

SWEEPS = 3
LOADW = 8


EMIN = 0.001
BETA = 0.5
LOWER = 0.06
UPPER = 3.0
patch_scale = 4.0


def extended(shard, sides, width):
    for axis, dim in sides:
        devices, length = (lax.axis_size(axis), shard.shape[dim])
        up = [(i, (i + 1) % devices) for i in range(devices - 1)]
        down = [(j, i) for i, j in up]
        last = lax.slice_in_dim(shard, length - width, length, axis=dim)
        first = lax.slice_in_dim(shard, 0, width, axis=dim)
        before = lax.ppermute(last, axis, up)
        after = lax.ppermute(first, axis, down)
        shard = jnp.concatenate([before, shard, after], axis=dim)
    return shard


def stencil_table():
    table = []
    for shift_x in (-1, 0, 1):
        for shift_y in (-1, 0, 1):
            for shift_z in (-1, 0, 1):
                reach = abs(shift_x) + abs(shift_y) + abs(shift_z)
                if reach > 0:
                    length = math.sqrt(reach)
                    coupling = 1.0 / 2 ** (reach - 1)
                    table.append(
                        (
                            shift_x,
                            shift_y,
                            shift_z,
                            coupling,
                            (shift_x / length, shift_y / length, shift_z / length),
                        )
                    )
    return table


def relaxations(count):
    middle = 0.5 * (UPPER + LOWER)
    radius = 0.5 * (UPPER - LOWER)
    return [
        1.0 / (middle + radius * math.cos(math.pi * (2 * index + 1) / (2 * count)))
        for index in range(count)
    ]


def pad_sides(array):
    widths = [(0, 0)] * (array.ndim - 2) + [(1, 1), (1, 1)]
    return jnp.pad(array, widths)


def neighbour(padded, shift_x, shift_y, shift_z, thick, rows, depth):
    return padded[
        ...,
        1 + shift_x : 1 + shift_x + thick,
        1 + shift_y : 1 + shift_y + rows,
        1 + shift_z : 1 + shift_z + depth,
    ]


def diagonal(root):
    padded = pad_sides(root)
    thick = root.shape[0] - 2
    rows = root.shape[1]
    depth = root.shape[2]
    centre = neighbour(padded, 0, 0, 0, thick, rows, depth)
    totals = [jnp.zeros((thick, rows, depth), jnp.float32) for axis_k in range(3)]
    for shift_x, shift_y, shift_z, coupling, normal in stencil_table():
        bond = coupling * centre * neighbour(padded, shift_x, shift_y, shift_z, thick, rows, depth)
        totals = [
            totals[axis_k] + bond * (1.0 + BETA * normal[axis_k] * normal[axis_k])
            for axis_k in range(3)
        ]
    return jnp.stack(totals)


def bond_terms(field, root, energy):
    parts_pad = [pad_sides(field[axis_k]) for axis_k in range(3)]
    root_pad = pad_sides(root)
    thick = field.shape[1] - 2
    rows = field.shape[2]
    depth = field.shape[3]
    centre_parts = [
        neighbour(parts_pad[axis_k], 0, 0, 0, thick, rows, depth) for axis_k in range(3)
    ]
    centre_root = neighbour(root_pad, 0, 0, 0, thick, rows, depth)
    total = jnp.zeros((thick, rows, depth), jnp.float32)
    totals = [jnp.zeros((thick, rows, depth), jnp.float32) for axis_k in range(3)]
    for shift_x, shift_y, shift_z, coupling, normal in stencil_table():
        bond = (
            coupling
            * centre_root
            * neighbour(root_pad, shift_x, shift_y, shift_z, thick, rows, depth)
        )
        differ = [
            centre_parts[axis_k]
            - neighbour(parts_pad[axis_k], shift_x, shift_y, shift_z, thick, rows, depth)
            for axis_k in range(3)
        ]
        along = None
        for axis_k in range(3):
            if normal[axis_k] != 0.0:
                term = normal[axis_k] * differ[axis_k]
                along = term if along is None else along + term
        forces = []
        for axis_k in range(3):
            if normal[axis_k] != 0.0:
                forces.append(differ[axis_k] + BETA * normal[axis_k] * along)
            else:
                forces.append(differ[axis_k])
        if energy:
            total = total + bond * (
                differ[0] * forces[0] + differ[1] * forces[1] + differ[2] * forces[2]
            )
        else:
            totals = [totals[axis_k] + bond * forces[axis_k] for axis_k in range(3)]
    if energy:
        return total
    return jnp.stack(totals)


def relax(field, root, diag, force, free, omega):
    product = bond_terms(field, root, False)
    return field[:, 1:-1] + omega * free * (force - product) / diag


def trim(array, have, want, axis_n):
    cut = have - want
    if cut == 0:
        return array
    return lax.slice_in_dim(array, cut, array.shape[axis_n] - cut, axis=axis_n)


def widen(field):
    return (extended(field, (("space", 1),), 1), 1)


def shards(density, void_depth, supports, load_x, load_y, load_vectors):
    cells_x, band, depth = density.shape
    groups = lax.axis_size("case")
    slabs = lax.axis_size("space")
    rows = band * groups
    total_x = cells_x * slabs
    heights = lax.broadcasted_iota(jnp.int32, density.shape, 2)
    offset = heights - depth // 2
    hollow = (offset >= 0) & (offset < void_depth[:, :, None])
    solid = density * (1.0 - hollow.astype(jnp.float32))
    margin = 1
    slab = lax.all_gather(solid, "case", axis=1, tiled=True)
    widened = extended(slab, (("space", 0),), margin)
    places = (
        lax.axis_index("space") * cells_x
        - margin
        + lax.broadcasted_iota(jnp.int32, (cells_x + 2 * margin, 1, 1), 0)
    )
    inside = (places >= 0) & (places < total_x)
    cubed_wide = widened * widened * widened
    root = jnp.where(inside, jnp.sqrt(EMIN + (1.0 - EMIN) * cubed_wide), 0.0)
    base = margin - 1
    inner = places[1:-1]
    inner_inside = ((inner >= 0) & (inner < total_x)).astype(jnp.float32)
    diag = diagonal(root)
    diag_safe = diag + (1.0 - inner_inside)
    inner_shape = (cells_x + 2 * base, rows, depth)
    heights_ext = lax.broadcasted_iota(jnp.int32, inner_shape, 2)
    lateral = lax.broadcasted_iota(jnp.int32, inner_shape, 1)
    support = supports[0]
    pinned = (heights_ext == 0) & ((inner < support[0]) | (inner >= total_x - support[1]))
    free = inner_inside * (1.0 - pinned.astype(jnp.float32))
    corner_x = load_x[0]
    corner_y = load_y[0]
    patch = (
        (heights_ext == depth - 1)
        & (inner >= corner_x)
        & (inner < corner_x + LOADW)
        & (lateral >= corner_y)
        & (lateral < corner_y + LOADW)
    )
    solid_inner = widened[1:-1]
    profile = load_vectors[0]
    first_plane = lax.axis_index("space") * cells_x
    planes = lax.dynamic_slice_in_dim(profile, first_plane, cells_x + 2 * base, 1)
    force = (free * (solid_inner + patch_scale * patch.astype(jnp.float32)))[None] * planes[
        :, :, None, None
    ]
    omegas = relaxations(SWEEPS)
    field = omegas[0] * free * force / diag_safe
    extent = base
    for index in range(1, SWEEPS):
        field, extent = widen(field)
        target = extent - 1
        field = relax(
            field,
            trim(root, margin, extent, 0),
            trim(diag_safe, base, target, 1),
            trim(force, base, target, 1),
            trim(free, base, target, 0),
            omegas[index],
        )
        extent = target
    field, extent = widen(field)
    energy = bond_terms(trim(field, extent, 1, 1), trim(root, margin, 1, 0), True)
    share = lax.psum_scatter(energy, "case", scatter_dimension=1, tiled=True)
    cubed = solid * solid * solid
    stiff = EMIN + (1.0 - EMIN) * cubed
    factor = -1.5 * (1.0 - EMIN) * solid * solid / stiff
    return (trim(field, extent, 0, 1)[None], factor * share / groups)


def solution(mesh):
    return jax.shard_map(
        shards,
        mesh=mesh,
        in_specs=(
            P("space", "case", None),
            P("space", "case"),
            P("case", None),
            P("case"),
            P("case"),
            P("case", None, None),
        ),
        out_specs=(P("case", None, "space", None, None), P("space", "case", None)),
        check_vma=False,
    )
```

profile of v0, /device:TPU:0, one launch (start us, length us, event | category | flops | bytes accessed | tf_op | source)
XLA Modules:
  0.0 91.8 jit_solution(3233868291165415508)
XLA Ops:
  7.2 0.8 subtract_multiply_fusion.1
  8.1 10.2 %all_gather.3 = f32[6,32,128]{2,1,0:T(8,128)S(1)} all-gather(f32[6,8,128]{2,1,0:T(8,128)S(1)} %subtract_multiply_fusion.1), channel_id=1, replica_groups=mesh['case'=4,'space'=8] {'case'}, dimensions={1}, use_global_device_ids=true | all-gather | bytes 122880 | tf_op jit(solution)/shard_map/all_gather | solution.py:164
  18.3 1.3 %collective-permute-start.1 = (f32[1,32,128]{2,1,0:T(8,128)S(1)}, f32[1,32,128]{2,1,0:T(8,128)S(1)}, u32[]{:S(2)}, u32[]{:S(2)}) collective-permute-start(f32[1,32,128]{2,1,0:T(8,128)S(1)} %get-tuple-element.52), channel_id=1, source_target_pairs={{1,0},{2,1},{3,2},{4,3},{5,4},{6,5},{7,6},{9,8},{10,9},{11,10},{12... | collective-permute-start | bytes 49160 | tf_op jit(solution)/shard_map/ppermute | solution.py:27
  19.5 3.0 %collective-permute-start = (f32[1,32,128]{2,1,0:T(8,128)S(1)}, f32[1,32,128]{2,1,0:T(8,128)S(1)}, u32[]{:S(2)}, u32[]{:S(2)}) collective-permute-start(f32[1,32,128]{2,1,0:T(8,128)S(1)} %get-tuple-element.53), channel_id=1, source_target_pairs={{0,1},{1,2},{2,3},{3,4},{4,5},{5,6},{6,7},{8,9},{9,10},{10,11},{11... | collective-permute-start | bytes 49160 | tf_op jit(solution)/shard_map/ppermute | solution.py:26
  25.9 0.7 or_bitcast_fusion
  28.1 3.1 %collective-permute-start.2 = (f32[3,1,32,128]{3,2,1,0:T(8,128)S(1)}, f32[3,1,32,128]{3,2,1,0:T(8,128)S(1)}, u32[]{:S(2)}, u32[]{:S(2)}) collective-permute-start(f32[3,1,32,128]{3,2,1,0:T(8,128)S(1)} %get-tuple-element.48), channel_id=1, source_target_pairs={{0,1},{1,2},{2,3},{3,4},{4,5},{5,6},{6,7},{8,9},{9,10},{10,11},{11... | collective-permute-start | bytes 147464 | tf_op jit(solution)/shard_map/ppermute | solution.py:26
  31.3 1.3 %collective-permute-start.3 = (f32[3,1,32,128]{3,2,1,0:T(8,128)S(1)}, f32[3,1,32,128]{3,2,1,0:T(8,128)S(1)}, u32[]{:S(2)}, u32[]{:S(2)}) collective-permute-start(f32[3,1,32,128]{3,2,1,0:T(8,128)S(1)} %get-tuple-element.49), channel_id=1, source_target_pairs={{1,0},{2,1},{3,2},{4,3},{5,4},{6,5},{7,6},{9,8},{10,9},{11,10},{12... | collective-permute-start | bytes 147464 | tf_op jit(solution)/shard_map/ppermute | solution.py:27
  32.6 1.8 %collective-permute-done.3 = f32[3,1,32,128]{3,2,1,0:T(8,128)S(1)} collective-permute-done((f32[3,1,32,128]{3,2,1,0:T(8,128)S(1)}, f32[3,1,32,128]{3,2,1,0:T(8,128)S(1)}, u32[]{:S(2)}, u32[]{:S(2)}) %collective-permute-start.3) | collective-permute-done | bytes 49184 | tf_op jit(solution)/shard_map/ppermute | solution.py:27
  34.4 1.1 %fusion.40 = (f32[6,32,128]{2,1,0:T(8,128)S(1)}, f32[6,32,128]{2,1,0:T(8,128)S(1)}, f32[6,32,128]{2,1,0:T(8,128)S(1)}) fusion(f32[6,32,128]{2,1,0:T(8,128)S(1)} %get-tuple-element.26, f32[6,32,128]{2,1,0:T(8,128)S(1)} %get-tuple-element.33, f32[6,32,128]{2,1,0:T(8,128)S(1)} %get-tuple-element.21, f32[8,32,128]{2,1,0:T(8,128)S(1)} %get-tuple-element.43, ...), kind=kLoop, calls=%fused_computation.367 | loop fusion | flops 4644864 | bytes 3932160 | tf_op jit(solution)/shard_map/add | solution.py:131
  35.6 1.1 %fusion.74 = f32[6,32,128]{2,1,0:T(8,128)S(1)} fusion(f32[6,32,128]{2,1,0:T(8,128)S(1)} %get-tuple-element.29, f32[6,32,128]{2,1,0:T(8,128)S(1)} %get-tuple-element.30, f32[6,32,128]{2,1,0:T(8,128)S(1)} %get-tuple-element.25, f32[8,32,128]{2,1,0:T(8,128)S(1)} %get-tuple-element.42, f32[6,32,128]{2,1,0:T(8,128)S(1)} %get-tuple-element.27, ...), kind=kLoop, calls=%fused_computation.401 | loop fusion | flops 4300800 | bytes 3932160 | tf_op jit(solution)/shard_map/add | solution.py:131
  36.6 1.0 %fusion.58 = f32[6,32,128]{2,1,0:T(8,128)S(1)} fusion(f32[6,32,128]{2,1,0:T(8,128)S(1)} %get-tuple-element.28, f32[6,32,128]{2,1,0:T(8,128)S(1)} %get-tuple-element.31, f32[6,32,128]{2,1,0:T(8,128)S(1)} %get-tuple-element.17, f32[8,32,128]{2,1,0:T(8,128)S(1)} %get-tuple-element.41, f32[6,32,128]{2,1,0:T(8,128)S(1)} %get-tuple-element.18, ...), kind=kLoop, calls=%fused_computation.385 | loop fusion | flops 4300800 | bytes 3932160 | tf_op jit(solution)/shard_map/add | solution.py:131
  37.8 4.7 %collective-permute-start.4 = (f32[3,1,32,128]{3,2,1,0:T(8,128)S(1)}, f32[3,1,32,128]{3,2,1,0:T(8,128)S(1)}, u32[]{:S(2)}, u32[]{:S(2)}) collective-permute-start(f32[3,1,32,128]{3,2,1,0:T(8,128)S(1)} %get-tuple-element.46), channel_id=1, source_target_pairs={{0,1},{1,2},{2,3},{3,4},{4,5},{5,6},{6,7},{8,9},{9,10},{10,11},{11... | collective-permute-start | bytes 147464 | tf_op jit(solution)/shard_map/ppermute | solution.py:26
  42.5 1.3 %collective-permute-start.5 = (f32[3,1,32,128]{3,2,1,0:T(8,128)S(1)}, f32[3,1,32,128]{3,2,1,0:T(8,128)S(1)}, u32[]{:S(2)}, u32[]{:S(2)}) collective-permute-start(f32[3,1,32,128]{3,2,1,0:T(8,128)S(1)} %get-tuple-element.47), channel_id=1, source_target_pairs={{1,0},{2,1},{3,2},{4,3},{5,4},{6,5},{7,6},{9,8},{10,9},{11,10},{12... | collective-permute-start | bytes 147464 | tf_op jit(solution)/shard_map/ppermute | solution.py:27
  43.8 1.8 %collective-permute-done.5 = f32[3,1,32,128]{3,2,1,0:T(8,128)S(1)} collective-permute-done((f32[3,1,32,128]{3,2,1,0:T(8,128)S(1)}, f32[3,1,32,128]{3,2,1,0:T(8,128)S(1)}, u32[]{:S(2)}, u32[]{:S(2)}) %collective-permute-start.5) | collective-permute-done | bytes 49184 | tf_op jit(solution)/shard_map/ppermute | solution.py:27
  45.7 1.1 %fusion.98 = (f32[6,32,128]{2,1,0:T(8,128)S(1)}, f32[6,32,128]{2,1,0:T(8,128)S(1)}, f32[6,32,128]{2,1,0:T(8,128)S(1)}) fusion(f32[6,32,128]{2,1,0:T(8,128)S(1)} %get-tuple-element.26, f32[6,32,128]{2,1,0:T(8,128)S(1)} %get-tuple-element.33, f32[6,32,128]{2,1,0:T(8,128)S(1)} %get-tuple-element.21, f32[8,32,128]{2,1,0:T(8,128)S(1)} %get-tuple-element.40, ...), kind=kLoop, calls=%fused_computation.425 | loop fusion | flops 4644864 | bytes 3932160 | tf_op jit(solution)/shard_map/add | solution.py:131
  46.8 1.1 %fusion.132 = f32[6,32,128]{2,1,0:T(8,128)S(1)} fusion(f32[6,32,128]{2,1,0:T(8,128)S(1)} %get-tuple-element.29, f32[6,32,128]{2,1,0:T(8,128)S(1)} %get-tuple-element.30, f32[6,32,128]{2,1,0:T(8,128)S(1)} %get-tuple-element.25, f32[8,32,128]{2,1,0:T(8,128)S(1)} %get-tuple-element.39, f32[6,32,128]{2,1,0:T(8,128)S(1)} %get-tuple-element.27, ...), kind=kLoop, calls=%fused_computation.459 | loop fusion | flops 4300800 | bytes 3932160 | tf_op jit(solution)/shard_map/add | solution.py:131
  47.8 1.0 %fusion.116 = f32[6,32,128]{2,1,0:T(8,128)S(1)} fusion(f32[6,32,128]{2,1,0:T(8,128)S(1)} %get-tuple-element.28, f32[6,32,128]{2,1,0:T(8,128)S(1)} %get-tuple-element.31, f32[6,32,128]{2,1,0:T(8,128)S(1)} %get-tuple-element.17, f32[8,32,128]{2,1,0:T(8,128)S(1)} %get-tuple-element.38, f32[6,32,128]{2,1,0:T(8,128)S(1)} %get-tuple-element.18, ...), kind=kLoop, calls=%fused_computation.443 | loop fusion | flops 4300800 | bytes 3932160 | tf_op jit(solution)/shard_map/add | solution.py:131
  49.0 4.2 %collective-permute-start.6 = (f32[3,1,32,128]{3,2,1,0:T(8,128)S(1)}, f32[3,1,32,128]{3,2,1,0:T(8,128)S(1)}, u32[]{:S(2)}, u32[]{:S(2)}) collective-permute-start(f32[3,1,32,128]{3,2,1,0:T(8,128)S(1)} %get-tuple-element.44), channel_id=1, source_target_pairs={{0,1},{1,2},{2,3},{3,4},{4,5},{5,6},{6,7},{8,9},{9,10},{10,11},{11... | collective-permute-start | bytes 147464 | tf_op jit(solution)/shard_map/ppermute | solution.py:26
  53.2 1.3 %collective-permute-start.7 = (f32[3,1,32,128]{3,2,1,0:T(8,128)S(1)}, f32[3,1,32,128]{3,2,1,0:T(8,128)S(1)}, u32[]{:S(2)}, u32[]{:S(2)}) collective-permute-start(f32[3,1,32,128]{3,2,1,0:T(8,128)S(1)} %get-tuple-element.45), channel_id=1, source_target_pairs={{1,0},{2,1},{3,2},{4,3},{5,4},{6,5},{7,6},{9,8},{10,9},{11,10},{12... | collective-permute-start | bytes 147464 | tf_op jit(solution)/shard_map/ppermute | solution.py:27
  54.6 1.8 %collective-permute-done.7 = f32[3,1,32,128]{3,2,1,0:T(8,128)S(1)} collective-permute-done((f32[3,1,32,128]{3,2,1,0:T(8,128)S(1)}, f32[3,1,32,128]{3,2,1,0:T(8,128)S(1)}, u32[]{:S(2)}, u32[]{:S(2)}) %collective-permute-start.7) | collective-permute-done | bytes 49184 | tf_op jit(solution)/shard_map/ppermute | solution.py:27
  56.4 2.4 %fusion.225 = f32[6,32,128]{2,1,0:T(8,128)} fusion(f32[6,32,128]{2,1,0:T(8,128)S(1)} %get-tuple-element.20, f32[6,32,128]{2,1,0:T(8,128)S(1)} %get-tuple-element.13, f32[6,32,128]{2,1,0:T(8,128)S(1)} %get-tuple-element.34, f32[6,32,128]{2,1,0:T(8,128)S(1)} %get-tuple-element.14, f32[6,32,128]{2,1,0:T(8,128)S(1)} %get-tuple-element.33, ...), kind=kLoop, calls=%fused_computation.552 | loop fusion | flops 10149888 | bytes 3735552 | tf_op jit(solution)/shard_map/add | solution.py:127
  58.8 0.9 fusion.2
  59.8 23.7 %reduce-scatter.2.cloned.1.call-done = f32[6,8,128]{2,1,0:T(8,128)} async-done(((f32[6,32,128]{2,1,0:T(8,128)}), f32[6,8,128]{2,1,0:T(8,128)}) %reduce-scatter.2.cloned.1.call-update) | async-done | bytes 24592 | tf_op jit(solution)/shard_map/reduce_scatter | solution.py:218
  83.5 1.4 %fusion.672 = f32[6,8,128]{2,1,0:T(8,128)} fusion(f32[6,8,128]{2,1,0:T(8,128)} %reduce-scatter.2.cloned.1.call-done, f32[6,8,128]{2,1,0:T(8,128)S(1)} %copy-done.1, s32[6,8]{1,0:T(8,128)S(1)} %copy-done.2, s32[128]{0:T(128)S(1)} %iota_add_fusion, pred[128]{0:T(512)(128)(4,1)S(1)} %broadcast_compare_fusion), kind=kLoop, calls=%fused_computation.1080 | loop fusion | flops 86016 | bytes 74560 | tf_op jit(solution)/shard_map/div | solution.py:222
  (45 shorter events, 3.4 us)
Async XLA Ops:
  7.2 18.0 %copy-start = (f32[1,3,48]{2,0,1:T(1,128)S(1)}, f32[1,3,48]{2,0,1:T(1,128)}, u32[]{:S(2)}) copy-start(f32[1,3,48]{2,0,1:T(1,128)} %param.11) | copy-start | bytes 1732
  7.2 76.3 %reduce-scatter.2.cloned.1.call-start = ((), (), s32[]{:S(2)}) async-start(), calls=%async_computation.1 | async-start | bytes 122880 | tf_op jit(solution)/shard_map/reduce_scatter | solution.py:218
  18.3 8.5 %collective-permute-start.1 = (f32[1,32,128]{2,1,0:T(8,128)S(1)}, f32[1,32,128]{2,1,0:T(8,128)S(1)}, u32[]{:S(2)}, u32[]{:S(2)}) collective-permute-start(f32[1,32,128]{2,1,0:T(8,128)S(1)} %get-tuple-element.52), channel_id=1, source_target_pairs={{1,0},{2,1},{3,2},{4,3},{5,4},{6,5},{7,6},{9,8},{10,9},{11,10},{12... | collective-permute-start | bytes 49160 | tf_op jit(solution)/shard_map/ppermute | solution.py:27
  19.5 7.1 %collective-permute-start = (f32[1,32,128]{2,1,0:T(8,128)S(1)}, f32[1,32,128]{2,1,0:T(8,128)S(1)}, u32[]{:S(2)}, u32[]{:S(2)}) collective-permute-start(f32[1,32,128]{2,1,0:T(8,128)S(1)} %get-tuple-element.53), channel_id=1, source_target_pairs={{0,1},{1,2},{2,3},{3,4},{4,5},{5,6},{6,7},{8,9},{9,10},{10,11},{11... | collective-permute-start | bytes 49160 | tf_op jit(solution)/shard_map/ppermute | solution.py:26
  23.9 0.7 copy-start.3
  28.1 4.4 %collective-permute-start.2 = (f32[3,1,32,128]{3,2,1,0:T(8,128)S(1)}, f32[3,1,32,128]{3,2,1,0:T(8,128)S(1)}, u32[]{:S(2)}, u32[]{:S(2)}) collective-permute-start(f32[3,1,32,128]{3,2,1,0:T(8,128)S(1)} %get-tuple-element.48), channel_id=1, source_target_pairs={{0,1},{1,2},{2,3},{3,4},{4,5},{5,6},{6,7},{8,9},{9,10},{10,11},{11... | collective-permute-start | bytes 147464 | tf_op jit(solution)/shard_map/ppermute | solution.py:26
  31.3 3.1 %collective-permute-start.3 = (f32[3,1,32,128]{3,2,1,0:T(8,128)S(1)}, f32[3,1,32,128]{3,2,1,0:T(8,128)S(1)}, u32[]{:S(2)}, u32[]{:S(2)}) collective-permute-start(f32[3,1,32,128]{3,2,1,0:T(8,128)S(1)} %get-tuple-element.49), channel_id=1, source_target_pairs={{1,0},{2,1},{3,2},{4,3},{5,4},{6,5},{7,6},{9,8},{10,9},{11,10},{12... | collective-permute-start | bytes 147464 | tf_op jit(solution)/shard_map/ppermute | solution.py:27
  37.8 6.0 %collective-permute-start.4 = (f32[3,1,32,128]{3,2,1,0:T(8,128)S(1)}, f32[3,1,32,128]{3,2,1,0:T(8,128)S(1)}, u32[]{:S(2)}, u32[]{:S(2)}) collective-permute-start(f32[3,1,32,128]{3,2,1,0:T(8,128)S(1)} %get-tuple-element.46), channel_id=1, source_target_pairs={{0,1},{1,2},{2,3},{3,4},{4,5},{5,6},{6,7},{8,9},{9,10},{10,11},{11... | collective-permute-start | bytes 147464 | tf_op jit(solution)/shard_map/ppermute | solution.py:26
  42.5 3.1 %collective-permute-start.5 = (f32[3,1,32,128]{3,2,1,0:T(8,128)S(1)}, f32[3,1,32,128]{3,2,1,0:T(8,128)S(1)}, u32[]{:S(2)}, u32[]{:S(2)}) collective-permute-start(f32[3,1,32,128]{3,2,1,0:T(8,128)S(1)} %get-tuple-element.47), channel_id=1, source_target_pairs={{1,0},{2,1},{3,2},{4,3},{5,4},{6,5},{7,6},{9,8},{10,9},{11,10},{12... | collective-permute-start | bytes 147464 | tf_op jit(solution)/shard_map/ppermute | solution.py:27
  49.0 5.5 %collective-permute-start.6 = (f32[3,1,32,128]{3,2,1,0:T(8,128)S(1)}, f32[3,1,32,128]{3,2,1,0:T(8,128)S(1)}, u32[]{:S(2)}, u32[]{:S(2)}) collective-permute-start(f32[3,1,32,128]{3,2,1,0:T(8,128)S(1)} %get-tuple-element.44), channel_id=1, source_target_pairs={{0,1},{1,2},{2,3},{3,4},{4,5},{5,6},{6,7},{8,9},{9,10},{10,11},{11... | collective-permute-start | bytes 147464 | tf_op jit(solution)/shard_map/ppermute | solution.py:26
  53.2 3.1 %collective-permute-start.7 = (f32[3,1,32,128]{3,2,1,0:T(8,128)S(1)}, f32[3,1,32,128]{3,2,1,0:T(8,128)S(1)}, u32[]{:S(2)}, u32[]{:S(2)}) collective-permute-start(f32[3,1,32,128]{3,2,1,0:T(8,128)S(1)} %get-tuple-element.45), channel_id=1, source_target_pairs={{1,0},{2,1},{3,2},{4,3},{5,4},{6,5},{7,6},{9,8},{10,9},{11,10},{12... | collective-permute-start | bytes 147464 | tf_op jit(solution)/shard_map/ppermute | solution.py:27
  58.8 24.6 %copy-start.1 = (f32[6,8,128]{2,1,0:T(8,128)S(1)}, f32[6,8,128]{2,1,0:T(8,128)}, u32[]{:S(2)}) copy-start(f32[6,8,128]{2,1,0:T(8,128)} %param.6) | copy-start | bytes 73732
  58.8 24.6 %copy-start.2 = (s32[6,8]{1,0:T(8,128)S(1)}, s32[6,8]{1,0:T(8,128)}, u32[]{:S(2)}) copy-start(s32[6,8]{1,0:T(8,128)} %param.7) | copy-start | bytes 580
Sparse Core Ops, SparseCore 0:
  58.9 24.4 reduce-scatter.1
where the time goes:
time: 92.2 us; the launch traced here: 91.8 us
  waiting for transfers between devices  29.2 us (32%)
  starting transfers between devices  20.2 us (22%)
  between operations  16.3 us (18%)
  other arithmetic  14.5 us (16%)
  blocking collectives  10.2 us (11%)
  local copies, waits for them, and re-layouts  1.37 us (1%)
    reduce_scatter x1, waiting for transfers between devices, shards(): share = lax.psum_scatter(energy, 'case', scatter_dimension=1, tiled=True)  23.7 us
    ppermute x4, starting transfers between devices, extended(): before = lax.ppermute(last, axis, up)  15 us
    all_gather x1, blocking collectives, shards(): slab = lax.all_gather(solid, 'case', axis=1, tiled=True)  10.2 us
    add x6, other arithmetic, bond_terms(): totals = [totals[axis_k] + bond * forces[axis_k] for axis_k in range(3)]  6.25 us
    ppermute x4, waiting for transfers between devices, extended(): after = lax.ppermute(first, axis, down)  5.45 us
    ppermute x4, starting transfers between devices, extended(): after = lax.ppermute(first, axis, down)  5.16 us
    add x1, other arithmetic, bond_terms(): total + bond * (differ[0] * forces[0] + differ[1] * forces[1] + differ[2]...  2.35 us
  transfers between devices with their start and end apart: 9, of which 4 were waited for; matrix products, arithmetic and copies ran while one was open for 3% of the time, Pallas kernels for 0%

commit v1 on v0

--- a/solution.py
+++ b/solution.py
@@ -146,10 +146,6 @@
     return lax.slice_in_dim(array, cut, array.shape[axis_n] - cut, axis=axis_n)
 
 
-def widen(field):
-    return (extended(field, (("space", 1),), 1), 1)
-
-
 def shards(density, void_depth, supports, load_x, load_y, load_vectors):
     cells_x, band, depth = density.shape
     groups = lax.axis_size("case")
@@ -160,9 +156,9 @@
     offset = heights - depth // 2
     hollow = (offset >= 0) & (offset < void_depth[:, :, None])
     solid = density * (1.0 - hollow.astype(jnp.float32))
-    margin = 1
-    slab = lax.all_gather(solid, "case", axis=1, tiled=True)
-    widened = extended(slab, (("space", 0),), margin)
+    margin = SWEEPS + 1
+    brick = extended(solid, (("space", 0),), margin)
+    widened = lax.all_gather(brick, "case", axis=1, tiled=True)
     places = (
         lax.axis_index("space") * cells_x
         - margin
@@ -194,6 +190,7 @@
     solid_inner = widened[1:-1]
     profile = load_vectors[0]
     first_plane = lax.axis_index("space") * cells_x
+    profile = jnp.pad(profile, ((0, 0), (base, base)))
     planes = lax.dynamic_slice_in_dim(profile, first_plane, cells_x + 2 * base, 1)
     force = (free * (solid_inner + patch_scale * patch.astype(jnp.float32)))[None] * planes[
         :, :, None, None
@@ -202,7 +199,6 @@
     field = omegas[0] * free * force / diag_safe
     extent = base
     for index in range(1, SWEEPS):
-        field, extent = widen(field)
         target = extent - 1
         field = relax(
             field,
@@ -213,9 +209,10 @@
             omegas[index],
         )
         extent = target
-    field, extent = widen(field)
     energy = bond_terms(trim(field, extent, 1, 1), trim(root, margin, 1, 0), True)
-    share = lax.psum_scatter(energy, "case", scatter_dimension=1, tiled=True)
+    pieces = energy.reshape(cells_x, groups, band, depth).transpose(1, 0, 2, 3)
+    swapped = lax.all_to_all(pieces, "case", split_axis=0, concat_axis=0, tiled=True)
+    share = jnp.sum(swapped, axis=0)
     cubed = solid * solid * solid
     stiff = EMIN + (1.0 - EMIN) * cubed
     factor = -1.5 * (1.0 - EMIN) * solid * solid / stiff

time: 92.2 us -> 52.4 us (0.57)
  waiting for transfers between devices: 29.2 us -> 4.17 us
  between operations: 16.3 us -> 2.84 us
  starting transfers between devices: 20.2 us -> 7.63 us
  other arithmetic: 14.5 us -> 21.6 us
  local copies, waits for them, and re-layouts: 1.37 us -> 3.49 us
  blocking collectives: 10.2 us -> 12.3 us
    reduce_scatter x1 -> x0, waiting for transfers between devices: 23.7 us -> none  [shards(): share = lax.psum_scatter(energy, 'case', scatter_dimension=1, tiled=True)]
    ppermute x4 -> x1, starting transfers between devices: 15 us -> 3.03 us  [extended(): before = lax.ppermute(last, axis, up)]
    another operation x0 -> x5, other arithmetic: none -> 10.3 us  [the longest x4 9.33 us: bond_terms(): return jnp.stack(totals)]
    add x10 -> x0, other arithmetic: 9.69 us -> none  [the longest x6 6.25 us: bond_terms(): totals = [totals[axis_k] + bond * forces[axis_k] for axis_k in range(3)]]
    slice x0 -> x3, other arithmetic: none -> 5.87 us  [neighbour(): padded[..., 1 + shift_x:1 + shift_x + thick, 1 + shift_y:1 + shift_y + ro...]
    ppermute x4 -> x1, waiting for transfers between devices: 5.45 us -> 0.01 us  [extended(): after = lax.ppermute(first, axis, down)]
    all_to_all x0 -> x1, waiting for transfers between devices: none -> 4.16 us  [shards(): lax.all_to_all(pieces, 'case', split_axis=0, concat_axis=0, tiled=True)]
    ppermute x4 -> x1, starting transfers between devices: 5.16 us -> 1.29 us  [extended(): after = lax.ppermute(first, axis, down)]
  transfers between devices with their start and end apart: 9 -> 3, of which waited for: 4 -> 1; matrix products, arithmetic and copies ran while one was open for 3% -> 4% of each run, Pallas kernels for 0% -> 0%
where the time goes in v1:
time: 52.4 us; the launch traced here: 52 us
  other arithmetic  21.6 us (41%)
  blocking collectives  12.3 us (23%)
  starting transfers between devices  7.63 us (15%)
  waiting for transfers between devices  4.17 us (8%)
  local copies, waits for them, and re-layouts  3.49 us (7%)
  between operations  2.84 us (5%)
    all_gather x1, blocking collectives, shards(): widened = lax.all_gather(brick, 'case', axis=1, tiled=True)  12.3 us
    another operation x4, other arithmetic, bond_terms(): return jnp.stack(totals)  9.33 us
    slice x3, other arithmetic, neighbour(): padded[..., 1 + shift_x:1 + shift_x + thick, 1 + shift_y:1 + shift_y + ro...  5.87 us
    all_to_all x1, waiting for transfers between devices, shards(): lax.all_to_all(pieces, 'case', split_axis=0, concat_axis=0, tiled=True)  4.16 us
    all_to_all x1, starting transfers between devices, shards(): lax.all_to_all(pieces, 'case', split_axis=0, concat_axis=0, tiled=True)  3.3 us
    ppermute x1, starting transfers between devices, extended(): before = lax.ppermute(last, axis, up)  3.03 us
    transpose x1, other arithmetic, shards(): pieces = energy.reshape(cells_x, groups, band, depth).transpose(1, 0, 2, 3)  2.19 us
    unnamed x9, local copies, waits for them, and re-layouts  1.32 us
  transfers between devices with their start and end apart: 3, of which 1 were waited for; matrix products, arithmetic and copies ran while one was open for 4% of the time, Pallas kernels for 0%

profile of v1, /device:TPU:0, one launch (start us, length us, event | category | flops | bytes accessed | tf_op | source)
XLA Modules:
  0.0 52.0 jit_solution(8154934762550093863)
XLA Ops:
  0.7 0.8 %subtract_multiply_fusion.1 = f32[6,8,128]{2,1,0:T(8,128)S(1)} fusion(f32[6,8,128]{2,1,0:T(8,128)} %param.6, s32[6,8]{1,0:T(8,128)} %param.7, s32[128]{0:T(128)S(1)} %iota_add_fusion, pred[128]{0:T(512)(128)(4,1)S(1)} %broadcast_compare_fusion), kind=kLoop, calls=%fused_computation.1232 | loop fusion | flops 30720 | bytes 49984 | tf_op jit(solution)/shard_map/mul | solution.py:158
  1.5 1.3 %collective-permute-start.1 = (f32[4,8,128]{2,1,0:T(8,128)S(1)}, f32[4,8,128]{2,1,0:T(8,128)S(1)}, u32[]{:S(2)}, u32[]{:S(2)}) collective-permute-start(f32[4,8,128]{2,1,0:T(8,128)S(1)} %get-tuple-element.30), channel_id=1, source_target_pairs={{1,0},{2,1},{3,2},{4,3},{5,4},{6,5},{7,6},{9,8},{10,9},{11,10},{12... | collective-permute-start | bytes 49160 | tf_op jit(solution)/shard_map/ppermute | solution.py:27
  2.8 3.0 %collective-permute-start = (f32[4,8,128]{2,1,0:T(8,128)S(1)}, f32[4,8,128]{2,1,0:T(8,128)S(1)}, u32[]{:S(2)}, u32[]{:S(2)}) collective-permute-start(f32[4,8,128]{2,1,0:T(8,128)S(1)} %get-tuple-element.29), channel_id=1, source_target_pairs={{0,1},{1,2},{2,3},{3,4},{4,5},{5,6},{6,7},{8,9},{9,10},{10,11},{11... | collective-permute-start | bytes 49160 | tf_op jit(solution)/shard_map/ppermute | solution.py:26
  6.5 0.6 %copy-done.2 = s32[1,2]{1,0:T(1,128)S(1)} copy-done((s32[1,2]{1,0:T(1,128)S(1)}, s32[1,2]{1,0:T(1,128)}, u32[]{:S(2)}) %copy-start.2) | copy-done | bytes 32
  7.2 0.6 %fusion.741 = (s32[1,1]{1,0:T(1,128)}, s32[1,1]{1,0:T(1,128)}) fusion(s32[1,2]{1,0:T(1,128)S(1)} %copy-done.2), kind=kLoop, calls=%fused_computation.1253 | loop fusion | bytes 16 | tf_op jit(solution)/shard_map/slice | solution.py:179
  8.4 0.7 %copy-done.3 = f32[1,3,48]{2,0,1:T(1,128)S(1)} copy-done((f32[1,3,48]{2,0,1:T(1,128)S(1)}, f32[1,3,48]{2,0,1:T(1,128)}, u32[]{:S(2)}) %copy-start.3) | copy-done | bytes 600
  9.9 0.7 %compare_bitcast_fusion.1 = (pred[12]{0:T(512)(128)(4,1)S(1)}, f32[12]{0:T(128)S(1)}, pred[12]{0:T(512)(128)(4,1)S(1)}, pred[12]{0:T(512)(128)(4,1)S(1)}) fusion(s32[]{:T(128)} %bitcast.683, s32[14,1,1]{0,2,1:T(1,128)S(1)} %iota_add_fusion.1, s32[]{:T(128)S(6)} %add.1734, s32[]{:T(128)} %bitcast.2, s32[]{:T(128)} %bitcast.1), kind=kLoop, calls=%fused_computation.1237 | loop fusion | flops 108 | bytes 148 | tf_op jit(solution)/shard_map/and | solution.py:184
  10.7 12.3 %all_gather.3 = f32[14,32,128]{2,1,0:T(8,128)S(1)} all-gather(f32[14,8,128]{2,1,0:T(8,128)S(1)} %pad_maximum_fusion), channel_id=1, replica_groups=mesh['case'=4,'space'=8] {'case'}, dimensions={1}, use_global_device_ids=true | all-gather | bytes 286720 | tf_op jit(solution)/shard_map/all_gather | solution.py:161
  23.0 1.0 %add_bitcast_fusion.2 = (f32[1,12,32,128]{3,2,1,0:T(8,128)S(1)}, f32[12,32,128]{2,1,0:T(8,128)S(1)}) fusion(f32[14,32,128]{2,1,0:T(8,128)S(1)} %fusion.7), kind=kLoop, calls=%fused_computation.382 | loop fusion | flops 3489792 | bytes 1212416 | tf_op jit(solution)/shard_map/stack | solution.py:89
  24.0 1.8 %fusion.739 = (f32[12,32,128]{2,1,0:T(8,128)S(1)}, f32[1,12,32,128]{3,2,1,0:T(8,128)S(1)}, f32[1,12,32,128]{3,2,1,0:T(8,128)S(1)}) fusion(f32[14,32,128]{2,1,0:T(8,128)S(1)} %fusion.7, f32[12,32,128]{2,1,0:T(8,128)S(1)} %get-tuple-element.11), kind=kLoop, calls=%fused_computation.1251 | loop fusion | flops 6389760 | bytes 1605632 | tf_op jit(solution)/shard_map/slice | solution.py:68
  26.0 0.2 multiply_divide_fusion
  26.2 2.9 %fusion.274 = (f32[1,10,32,128]{3,2,1,0:T(8,128)S(1)}, f32[10,32,128]{2,1,0:T(8,128)S(1)}, f32[10,32,128]{2,1,0:T(8,128)S(1)}) fusion(f32[3,12,32,128]{3,2,1,0:T(8,128)S(1)} %get-tuple-element.8, f32[12,32,128]{2,1,0:T(8,128)S(1)} %get-tuple-element.14, f32[12,32,128]{2,1,0:T(8,128)S(1)} %get-tuple-element.12, f32[12,32,128]{2,1,0:T(8,128)S(1)} %get-tuple-element.13, ...), kind=kLoop, calls=%fused_computation.653 | loop fusion | flops 8806400 | bytes 2588672 | tf_op jit(solution)/shard_map/stack | solution.py:134
  29.1 2.4 %fusion.272 = f32[1,10,32,128]{3,2,1,0:T(8,128)S(1)} fusion(f32[12,32,128]{2,1,0:T(8,128)S(1)} %get-tuple-element.13, f32[10,32,128]{2,1,0:T(8,128)S(1)} %get-tuple-element.7, f32[3,12,32,128]{3,2,1,0:T(8,128)S(1)} %get-tuple-element.8, f32[10,32,128]{2,1,0:T(8,128)S(1)} %get-tuple-element.6, f32[12,32,128]{2,1,0:T(8,128)S(1)} %get-tuple-element.12, ...), kind=kLoop, calls=%fused_computation.651 | loop fusion | flops 8232960 | bytes 2588672 | tf_op jit(solution)/shard_map/stack | solution.py:134
  31.6 2.3 %fusion.738 = (f32[10,32,128]{2,1,0:T(8,128)S(1)}, f32[1,10,32,128]{3,2,1,0:T(8,128)S(1)}) fusion(f32[14,32,128]{2,1,0:T(8,128)S(1)} %fusion.7, f32[10,32,128]{2,1,0:T(8,128)S(1)} %get-tuple-element.7, f32[3,12,32,128]{3,2,1,0:T(8,128)S(1)} %get-tuple-element.8, f32[10,32,128]{2,1,0:T(8,128)S(1)} %get-tuple-element.6, ...), kind=kLoop, calls=%fused_computation.1250 | loop fusion | flops 8232960 | bytes 2752512 | tf_op jit(solution)/shard_map/slice | solution.py:68
  33.9 0.2 fusion
  34.2 2.0 %fusion.508 = (f32[1,8,32,128]{3,2,1,0:T(8,128)S(1)}, f32[8,32,128]{2,1,0:T(8,128)S(1)}, f32[8,32,128]{2,1,0:T(8,128)S(1)}) fusion(f32[3,10,32,128]{3,2,1,0:T(8,128)S(1)} %fusion, f32[10,32,128]{2,1,0:T(8,128)S(1)} %get-tuple-element.17, f32[10,32,128]{2,1,0:T(8,128)S(1)} %get-tuple-element.15, f32[10,32,128]{2,1,0:T(8,128)S(1)} %get-tuple-element.16, ...), kind=kLoop, calls=%fused_computation.976 | loop fusion | flops 7045120 | bytes 2097152 | tf_op jit(solution)/shard_map/stack | solution.py:134
  36.2 2.0 %fusion.506 = f32[1,8,32,128]{3,2,1,0:T(8,128)S(1)} fusion(f32[10,32,128]{2,1,0:T(8,128)S(1)} %get-tuple-element.16, f32[8,32,128]{2,1,0:T(8,128)S(1)} %get-tuple-element.4, f32[3,10,32,128]{3,2,1,0:T(8,128)S(1)} %fusion, f32[8,32,128]{2,1,0:T(8,128)S(1)} %get-tuple-element.3, f32[10,32,128]{2,1,0:T(8,128)S(1)} %get-tuple-element.15, ...), kind=kLoop, calls=%fused_computation.974 | loop fusion | flops 6586368 | bytes 2097152 | tf_op jit(solution)/shard_map/stack | solution.py:134
  38.2 1.8 %fusion.737 = (f32[8,32,128]{2,1,0:T(8,128)S(1)}, f32[1,8,32,128]{3,2,1,0:T(8,128)S(1)}) fusion(f32[14,32,128]{2,1,0:T(8,128)S(1)} %fusion.7, f32[8,32,128]{2,1,0:T(8,128)S(1)} %get-tuple-element.4, f32[3,10,32,128]{3,2,1,0:T(8,128)S(1)} %fusion, f32[8,32,128]{2,1,0:T(8,128)S(1)} %get-tuple-element.3, f32[10,32,128]{2,1,0:T(8,128)S(1)} %get-tuple-element.16, ...), kind=kLoop, calls=%fused_computation.1249 | loop fusion | flops 6586368 | bytes 2228224 | tf_op jit(solution)/shard_map/slice | solution.py:68
  40.2 2.2 %fusion.602 = f32[4,6,8,128]{3,2,0,1:T(8,128)S(1)} fusion(f32[8,32,128]{2,1,0:T(8,128)S(1)} %get-tuple-element.21, f32[8,32,128]{2,1,0:T(8,128)S(1)} %get-tuple-element.20, f32[8,32,128]{2,1,0:T(8,128)S(1)} %get-tuple-element.19, f32[8,32,128]{2,1,0:T(8,128)S(1)} %get-tuple-element.18, f32[3,8,32,128]{3,2,1,0:T(8,128)S(1)} %fusion.2, ...), kind=kLoop, calls=%fused_computation.1070 | loop fusion | flops 10690560 | bytes 1802240 | tf_op jit(solution)/shard_map/transpose | solution.py:213
  42.4 0.6 %copy.8 = f32[4,6,8,128]{3,2,1,0:T(8,128)} copy(f32[4,6,8,128]{3,2,0,1:T(8,128)S(1)} %fusion.602) | data formatting | bytes 196608 | tf_op jit(solution)/shard_map/transpose | solution.py:213
  43.1 3.3 %all-to-all-start = ((f32[4,6,8,128]{3,2,1,0:T(8,128)}), f32[4,6,8,128]{3,2,1,0:T(8,128)S(1)}, u32[]{:S(2)}, u32[]{:S(2)}) async-start(f32[4,6,8,128]{3,2,1,0:T(8,128)} %copy.8), calls=%async_computation | async-start | bytes 196608 | tf_op jit(solution)/shard_map/all_to_all | solution.py:214
  46.4 0.7 %slice_bitcast_fusion = f32[1,3,6,32,128]{4,3,2,1,0:T(8,128)} fusion(f32[3,8,32,128]{3,2,1,0:T(8,128)S(1)} %fusion.2), kind=kLoop, calls=%fused_computation.323 | loop fusion | bytes 589824 | tf_op jit(solution)/shard_map/broadcast_in_dim | solution.py:219
  47.1 4.2 %all-to-all-done = f32[4,6,8,128]{3,2,1,0:T(8,128)S(1)} async-done(((f32[4,6,8,128]{3,2,1,0:T(8,128)}), f32[4,6,8,128]{3,2,1,0:T(8,128)S(1)}, u32[]{:S(2)}, u32[]{:S(2)}) %all-to-all-start) | async-done | bytes 98336 | tf_op jit(solution)/shard_map/all_to_all | solution.py:214
  51.3 0.7 %fusion.733 = f32[6,8,128]{2,1,0:T(8,128)} fusion(f32[6,8,128]{2,1,0:T(8,128)S(1)} %reduce_sum.9, f32[6,8,128]{2,1,0:T(8,128)S(1)} %copy-done, s32[6,8]{1,0:T(8,128)S(1)} %copy-done.1, s32[128]{0:T(128)S(1)} %iota_add_fusion, pred[128]{0:T(512)(128)(4,1)S(1)} %broadcast_compare_fusion), kind=kLoop, calls=%fused_computation.1229 | loop fusion | flops 86016 | bytes 74560 | tf_op jit(solution)/shard_map/div | solution.py:219
  (28 shorter events, 0.8 us)
Async XLA Ops:
  1.5 9.1 %collective-permute-start.1 = (f32[4,8,128]{2,1,0:T(8,128)S(1)}, f32[4,8,128]{2,1,0:T(8,128)S(1)}, u32[]{:S(2)}, u32[]{:S(2)}) collective-permute-start(f32[4,8,128]{2,1,0:T(8,128)S(1)} %get-tuple-element.30), channel_id=1, source_target_pairs={{1,0},{2,1},{3,2},{4,3},{5,4},{6,5},{7,6},{9,8},{10,9},{11,10},{12... | collective-permute-start | bytes 49160 | tf_op jit(solution)/shard_map/ppermute | solution.py:27
  2.8 7.8 %collective-permute-start = (f32[4,8,128]{2,1,0:T(8,128)S(1)}, f32[4,8,128]{2,1,0:T(8,128)S(1)}, u32[]{:S(2)}, u32[]{:S(2)}) collective-permute-start(f32[4,8,128]{2,1,0:T(8,128)S(1)} %get-tuple-element.29), channel_id=1, source_target_pairs={{0,1},{1,2},{2,3},{3,4},{4,5},{5,6},{6,7},{8,9},{9,10},{10,11},{11... | collective-permute-start | bytes 49160 | tf_op jit(solution)/shard_map/ppermute | solution.py:26
  6.5 0.7 %copy-start.2 = (s32[1,2]{1,0:T(1,128)S(1)}, s32[1,2]{1,0:T(1,128)}, u32[]{:S(2)}) copy-start(s32[1,2]{1,0:T(1,128)} %param.8) | copy-start | bytes 28
  8.4 0.7 %copy-start.3 = (f32[1,3,48]{2,0,1:T(1,128)S(1)}, f32[1,3,48]{2,0,1:T(1,128)}, u32[]{:S(2)}) copy-start(f32[1,3,48]{2,0,1:T(1,128)} %param.11) | copy-start | bytes 1732
  43.1 8.2 %all-to-all-start = ((f32[4,6,8,128]{3,2,1,0:T(8,128)}), f32[4,6,8,128]{3,2,1,0:T(8,128)S(1)}, u32[]{:S(2)}, u32[]{:S(2)}) async-start(f32[4,6,8,128]{3,2,1,0:T(8,128)} %copy.8), calls=%async_computation | async-start | bytes 196608 | tf_op jit(solution)/shard_map/all_to_all | solution.py:214
  47.1 4.2 %copy-start = (f32[6,8,128]{2,1,0:T(8,128)S(1)}, f32[6,8,128]{2,1,0:T(8,128)}, u32[]{:S(2)}) copy-start(f32[6,8,128]{2,1,0:T(8,128)} %param.6) | copy-start | bytes 73732
  47.1 4.2 %copy-start.1 = (s32[6,8]{1,0:T(8,128)S(1)}, s32[6,8]{1,0:T(8,128)}, u32[]{:S(2)}) copy-start(s32[6,8]{1,0:T(8,128)} %param.7) | copy-start | bytes 580
